TPU v7x, 32 devices: a whole 2x2x4 slice. The times are simulated.
32 devices in a mesh: dp: 4 (over x, core), tensor: 8 (over z, y).
Axes of the slice: x: 2, y: 2, z: 4, core: 2. Of those that a mesh axis runs over, the one named last changes fastest.
Arguments:
- tokens: bfloat16 [4096, 3072], P(('dp', 'tensor')), may hold values from -6 to 6
- routes: int32 [4096, 2], P(('dp', 'tensor')), may hold values from 0 to 7, as said below
- router: bfloat16 [3072, 8], replicated, may hold values from -0.109375 to 0.109375
- w_up: bfloat16 [3072, 16384], P('dp', 'tensor'), may hold values from -0.109375 to 0.109375
- w_down: bfloat16 [16384, 3072], P(('tensor', 'dp')), may hold values from -0.046875 to 0.046875
- grad_parts: bfloat16 [4, 16384, 3072], P('dp', 'tensor'), may hold values from -6 to 6
- master: float32 [16384, 3072], P(('tensor', 'dp')), may hold values from -4 to 4
- moment_one: bfloat16 [16384, 3072], P(('tensor', 'dp')), may hold values from -3 to 3
- moment_two: float32 [16384, 3072], P(('tensor', 'dp')), may hold values from 0.01 to 1
Outputs:
- mixed: bfloat16 [4096, 3072], P(('dp', 'tensor'))
- new_master: float32 [16384, 3072], P(('tensor', 'dp'))
- new_moment_one: bfloat16 [16384, 3072], P(('tensor', 'dp'))
- new_moment_two: float32 [16384, 3072], P(('tensor', 'dp'))
Inputs may be any that keep to these rules, and one draw needn't show every extreme that they name: `routes`: each row names two different experts. Among the 128 rows of one device at most 48 name expert 0, and on some device exactly 48.
All inputs are finite; a program needn't handle non-finite values.
Results may differ from a plain program's by a relative error of at most 0.02.
Values may be sent and summed in bfloat16 or wider, within the bound.
A program may use at most 128 MiB of HBM per device.

v0:
```python
import jax
import jax.numpy as jnp
from jax import lax
from jax.sharding import PartitionSpec as P

CAP = 48


beta_first = 0.9
beta_second = 0.999
learn_rate = 0.01
decay_rate = 0.1
adam_eps = 1e-08
bias_first = 1.0 - (0.9**10) ** 10
bias_second = 1.0 - (0.999**10) ** 10


def gating_of(tokens, routes, router):
    logits = jnp.dot(tokens, router, preferred_element_type=jnp.float32)
    expert_iota = jnp.arange(logits.shape[1], dtype=jnp.int32)
    chosen = jnp.sum(jnp.where(routes[:, :, None] == expert_iota, logits[:, None, :], 0.0), axis=2)
    is_first = routes[:, 0] == 0
    routed = is_first | (routes[:, 1] == 0)
    own_logit = jnp.where(is_first, chosen[:, 0], chosen[:, 1])
    partner = jnp.where(is_first, chosen[:, 1], chosen[:, 0])
    gating = jnp.where(routed, jax.nn.sigmoid(own_logit - partner), 0.0)
    return (routed, gating)


def adam_step(grad_total, master, moment_one, moment_two):
    new_one = (
        beta_first * moment_one.astype(jnp.float32) + (1.0 - beta_first) * grad_total
    ).astype(jnp.bfloat16)
    new_two = beta_second * moment_two + (1.0 - beta_second) * grad_total * grad_total
    update = new_one.astype(jnp.float32) / bias_first / (jnp.sqrt(new_two / bias_second) + adam_eps)
    new_master = master - learn_rate * (update + decay_rate * master)
    return (new_master, new_one, new_two)


def local(tokens, routes, router, w_up, w_down, grad_parts, master, moment_one, moment_two):
    routed, gating = gating_of(tokens, routes, router)
    slot_index = jnp.cumsum(routed.astype(jnp.int32)) - 1
    slot_iota = jnp.arange(CAP, dtype=jnp.int32)
    picks = ((slot_index[None, :] == slot_iota[:, None]) & routed[None, :]).astype(jnp.bfloat16)
    picked_rows = jnp.dot(picks, tokens, preferred_element_type=jnp.float32).astype(jnp.bfloat16)
    gathered = lax.all_gather(picked_rows, "tensor", axis=0, tiled=True)
    up_out = jnp.dot(
        gathered, lax.all_gather(w_up, "dp", axis=0, tiled=True), preferred_element_type=jnp.float32
    )
    hidden = jax.nn.gelu(up_out, approximate=False).astype(jnp.bfloat16)
    partials = jnp.dot(
        hidden, lax.all_gather(w_down, "dp", axis=0, tiled=True), preferred_element_type=jnp.float32
    )
    owned = lax.psum_scatter(
        partials.astype(jnp.bfloat16), "tensor", scatter_dimension=0, tiled=True
    ).astype(jnp.float32)
    combined = jnp.take(owned, jnp.clip(slot_index, 0, CAP - 1), axis=0)
    mixed = (combined * gating[:, None]).astype(jnp.bfloat16)
    local_grad = grad_parts[0]
    grad_total = lax.psum_scatter(local_grad, "dp", scatter_dimension=0, tiled=True).astype(
        jnp.float32
    )
    new_master, new_one, new_two = adam_step(grad_total, master, moment_one, moment_two)
    return (mixed, new_master, new_one, new_two)


def solution(mesh):
    placed = (
        P(("dp", "tensor"), None),
        P(("dp", "tensor"), None),
        P(),
        P("dp", "tensor"),
        P(("tensor", "dp"), None),
        P("dp", "tensor", None),
        P(("tensor", "dp"), None),
        P(("tensor", "dp"), None),
        P(("tensor", "dp"), None),
    )
    return jax.shard_map(
        local,
        mesh=mesh,
        in_specs=placed,
        out_specs=(
            P(("dp", "tensor"), None),
            P(("tensor", "dp"), None),
            P(("tensor", "dp"), None),
            P(("tensor", "dp"), None),
        ),
        check_vma=False,
    )
```

profile of v0, /device:TPU:0, one launch (start us, length us, event | category | flops | bytes accessed | tf_op | source)
XLA Modules:
  0.0 447.3 jit_solution(16891343700286603789)
XLA Ops:
  7.2 0.0 copy-start
  7.2 0.0 all-gather.4.cloned.1.call-start
  7.2 0.8 slice_compare_fusion
  8.0 0.1 copy.31
  8.1 0.1 copy.32
  8.3 0.1 or_reduce_fusion
  8.4 0.2 reduce-window.4
  8.6 0.1 fusion.44
  8.7 0.0 copy-done
  8.7 1.0 convolution_convert_fusion.1
  9.7 0.0 all-gather.4.cloned.1.call-update
  9.7 0.0 all-gather.6.cloned.1.call-start
  9.7 0.7 all-gather.6.cloned.1.call-update
  10.4 0.0 all-gather.8.cloned.1.call-start
  10.5 0.7 all-gather.8.cloned.1.call-update
  11.2 0.0 reduce-scatter.3.cloned.1.call-start
  11.2 54.4 %all-gather.4.cloned.1.call-done = bf16[384,3072]{1,0:T(8,128)(2,1)} async-done(((bf16[48,3072]{1,0:T(8,128)(2,1)}), bf16[384,3072]{1,0:T(8,128)(2,1)}) %all-gather.4.cloned.1.call-update) | async-done | bytes 2359312 | tf_op jit(solution)/shard_map/all_gather | solution.py:46
  65.6 82.2 %all-gather.6.cloned.1.call-done = bf16[3072,2048]{1,0:T(8,128)(2,1)} async-done(((bf16[768,2048]{1,0:T(8,128)(2,1)}), bf16[3072,2048]{1,0:T(8,128)(2,1)}) %all-gather.6.cloned.1.call-update) | async-done | bytes 12582928 | tf_op jit(solution)/shard_map/all_gather | solution.py:48
  147.8 83.7 %all-gather.8.cloned.1.call-done = bf16[2048,3072]{1,0:T(8,128)(2,1)} async-done(((bf16[512,3072]{1,0:T(8,128)(2,1)}), bf16[2048,3072]{1,0:T(8,128)(2,1)}) %all-gather.8.cloned.1.call-update) | async-done | bytes 12582928 | tf_op jit(solution)/shard_map/all_gather | solution.py:52
  231.5 26.7 %convolution_convert_fusion = bf16[384,3072]{1,0:T(8,128)(2,1)} fusion(bf16[2048,3072]{1,0:T(8,128)(2,1)} %all-gather.8.cloned.1.call-done, bf16[384,3072]{1,0:T(8,128)(2,1)} %all-gather.4.cloned.1.call-done, bf16[3072,2048]{1,0:T(8,128)(2,1)} %all-gather.6.cloned.1.call-done), kind=kOutput, calls=%fused_computation.8 | convolution fusion | flops 9715974144 | bytes 29884416 | tf_op jit(solution)/shard_map/dot_general | solution.py:51
  258.3 0.0 reduce-scatter.3.cloned.1.call-update
  258.3 0.0 reduce-scatter.5.cloned.1.call-start
  258.3 0.0 copy-start.1
  258.3 0.0 copy-start.2
  258.4 0.5 reduce-scatter.5.cloned.1.call-update
  258.9 0.3 copy-done.1
  259.1 0.3 fusion.84
  259.4 0.0 copy-done.2
  259.5 0.1 copy.34
  259.6 0.1 copy.35
  259.7 0.1 select_reduce_fusion
  259.9 67.6 %reduce-scatter.3.cloned.1.call-done = bf16[48,3072]{1,0:T(8,128)(2,1)} async-done(((bf16[384,3072]{1,0:T(8,128)(2,1)}), bf16[48,3072]{1,0:T(8,128)(2,1)}) %reduce-scatter.3.cloned.1.call-update) | async-done | bytes 294928 | tf_op jit(solution)/shard_map/reduce_scatter | solution.py:54
  327.5 1.0 convert_element_type.36
  328.5 1.2 gather_fusion
  329.6 1.1 multiply_convert_fusion
  330.8 97.2 %reduce-scatter.5.cloned.1.call-done = bf16[512,3072]{1,0:T(8,128)(2,1)} async-done(((bf16[2048,3072]{1,0:T(8,128)(2,1)}), bf16[512,3072]{1,0:T(8,128)(2,1)}) %reduce-scatter.5.cloned.1.call-update) | async-done | bytes 3145744 | tf_op jit(solution)/shard_map/reduce_scatter | solution.py:60
  428.0 12.8 %multiply_subtract_fusion = (f32[512,3072]{1,0:T(8,128)}, bf16[512,3072]{1,0:T(8,128)(2,1)}, f32[512,3072]{1,0:T(8,128)}) fusion(f32[512,3072]{1,0:T(8,128)} %param.15, bf16[512,3072]{1,0:T(8,128)(2,1)} %reduce-scatter.5.cloned.1.call-done, bf16[512,3072]{1,0:T(8,128)(2,1)} %param.16, f32[512,3072]{1,0:T(8,128)} %param.17), kind=kLoop, calls=%fused_computation.6 | loop fusion | flops 29884416 | bytes 34603008 | tf_op jit(solution)/shard_map/sub | solution.py:36
  (4 shorter events, 0.1 us)
Async XLA Ops:
  7.2 1.5 copy-start
  7.2 58.4 %all-gather.4.cloned.1.call-start = ((), (), s32[]{:S(2)}) async-start(), calls=%async_computation.2 | async-start | bytes 2654208 | tf_op jit(solution)/shard_map/all_gather | solution.py:46
  9.7 138.1 %all-gather.6.cloned.1.call-start = ((), (), s32[]{:S(2)}) async-start(), calls=%async_computation.3 | async-start | bytes 15728640 | tf_op jit(solution)/shard_map/all_gather | solution.py:48
  10.4 221.1 %all-gather.8.cloned.1.call-start = ((), (), s32[]{:S(2)}) async-start(), calls=%async_computation.4 | async-start | bytes 15728640 | tf_op jit(solution)/shard_map/all_gather | solution.py:52
  11.2 316.3 %reduce-scatter.3.cloned.1.call-start = ((), (), s32[]{:S(2)}) async-start(), calls=%async_computation.5 | async-start | bytes 2654208 | tf_op jit(solution)/shard_map/reduce_scatter | solution.py:54
  258.3 169.7 %reduce-scatter.5.cloned.1.call-start = ((), (), s32[]{:S(2)}) async-start(), calls=%async_computation.6 | async-start | bytes 15728640 | tf_op jit(solution)/shard_map/reduce_scatter | solution.py:60
  258.3 0.8 copy-start.1
  258.3 1.1 copy-start.2
Sparse Core Ops, SparseCore 0:
  10.8 54.7 all-gather.3
  67.1 80.6 all-gather.5
  149.4 82.0 all-gather.7
  258.4 69.0 reduce-scatter.2
  329.9 98.0 reduce-scatter.4
where the time goes:
time: 448 us; the launch traced here: 447 us
  waiting for transfers between devices  387 us (86%)
  matrix products  28 us (6%)
  other arithmetic  16.2 us (4%)
  between operations  13.9 us (3%)
    reduce_scatter x1, waiting for transfers between devices, local(): lax.psum_scatter(local_grad, 'dp', scatter_dimension=0, tiled=True)  97.2 us
    all_gather x1, waiting for transfers between devices, local(): lax.all_gather(w_down, 'dp', axis=0, tiled=True)  83.7 us
    all_gather x1, waiting for transfers between devices, local(): lax.all_gather(w_up, 'dp', axis=0, tiled=True)  82.2 us
    reduce_scatter x1, waiting for transfers between devices, local(): lax.psum_scatter(partials.astype(jnp.bfloat16), 'tensor', scatter_dimensi...  67.6 us
    all_gather x1, waiting for transfers between devices, local(): gathered = lax.all_gather(picked_rows, 'tensor', axis=0, tiled=True)  54.4 us
    dot_general x1, matrix products, local(): jnp.dot(hidden, lax.all_gather(w_down, 'dp', axis=0, tiled=True), preferr...  26.7 us
    sub x1, other arithmetic, adam_step(): new_master = master - learn_rate * (update + decay_rate * master)  12.8 us
  transfers between devices with their start and end apart: 5, of which 5 were waited for; matrix products, arithmetic and copies ran while one was open for 1% of the time, Pallas kernels for 0%

commit v1 on v0

--- a/solution.py
+++ b/solution.py
@@ -1,6 +1,10 @@
+import functools
+
 import jax
 import jax.numpy as jnp
 from jax import lax
+from jax.experimental import pallas as pl
+from jax.experimental.pallas import tpu as pltpu
 from jax.sharding import PartitionSpec as P
 
 CAP = 48
@@ -61,6 +65,313 @@
         jnp.float32
     )
     new_master, new_one, new_two = adam_step(grad_total, master, moment_one, moment_two)
+    return (mixed, new_master, new_one, new_two)
+
+
+CHUNKS = 8
+VMEM_BYTES = 60 * 1024 * 1024
+
+
+def flip(index, bit):
+    return index + bit - 2 * bit * lax.rem(lax.div(index, bit), 2)
+
+
+def layer_kernel(
+    n_dp, n_tensor, pk, wup_hbm, wdown_hbm, grad_hbm,
+    owned, gsum,
+    x, wup, up, up_near, up_cross, hid, wd, out, from_y, from_z, from_far, fin_out, fin_in,
+    g_own, g_near, g_cross, send_sem, recv_sem, local_sem,
+):
+    p = lax.axis_index("dp")
+    t = lax.axis_index("tensor")
+    c, h = lax.rem(p, 2), lax.div(p, 2)
+    z, y = lax.div(t, 2), lax.rem(t, 2)
+    p1, p2 = flip(p, 1), flip(p, 2)
+    p3 = flip(p1, 2)
+    t1, t2, t4 = flip(t, 1), flip(t, 2), flip(t, 4)
+    z1, z2 = flip(z, 1), flip(z, 2)
+    z3 = flip(z1, 2)
+    core, cross, diag = (p1, t), (p2, t), (p3, t)
+    side, near, far = (p, t1), (p, t2), (p, t4)
+    cap = pk.shape[1]
+    share = wdown_hbm.shape[0]
+    piece = share // CHUNKS
+    n_z = n_tensor // 2
+    used = [0]
+    sent = []
+
+    def send(src, dst, device):
+        k = used[0]
+        used[0] += 1
+        copy = pltpu.make_async_remote_copy(
+            src_ref=src, dst_ref=dst, send_sem=send_sem.at[k], recv_sem=recv_sem.at[k],
+            device_id=device, device_id_type=pl.DeviceIdType.MESH,
+        )
+        copy.start()
+        sent.append(copy)
+        return copy
+
+    barrier = pltpu.get_barrier_semaphore()
+    for device in (core, cross, diag, side, near, far):
+        pl.semaphore_signal(barrier, inc=1, device_id=device, device_id_type=pl.DeviceIdType.MESH)
+    pl.semaphore_wait(barrier, 6)
+
+    def rows_of(q):
+        return pl.ds(pl.multiple_of(q * cap, 16), cap)
+
+    def share_of(q):
+        return pl.ds(pl.multiple_of(q * share, 16), share)
+
+    tok = [
+        send(pk.at[p2], x.at[t, rows_of(p)], cross),
+        send(pk.at[p3], x.at[t, rows_of(p)], diag),
+        send(pk.at[p1], x.at[t, rows_of(p)], core),
+    ]
+    loads = [
+        pltpu.make_async_copy(pk.at[p], x.at[t, rows_of(p)], local_sem.at[0]),
+        pltpu.make_async_copy(wup_hbm, wup, local_sem.at[1]),
+        pltpu.make_async_copy(grad_hbm.at[0, share_of(p2)], g_own.at[0], local_sem.at[2]),
+        pltpu.make_async_copy(wdown_hbm, wd.at[c], local_sem.at[3]),
+        pltpu.make_async_copy(grad_hbm.at[0, share_of(p)], g_own.at[1], local_sem.at[4]),
+    ]
+    for load in loads:
+        load.start()
+    grad_core = [send(grad_hbm.at[0, share_of(p3)], g_near.at[0], core)]
+
+    for copy in tok:
+        copy.wait_recv()
+    loads[0].wait()
+
+    def pass_on(block, devices):
+        return [send(x.at[block], x.at[block], device) for device in devices]
+
+    tile = 512
+
+    def project(from_z_at, s):
+        block = 2 * from_z_at + (y if s == 1 else 1 - y)
+
+        @pl.loop(0, 2)
+        def _(part):
+            for j in range(up.shape[5] // tile):
+                start = pl.multiple_of(part * up.shape[5] + j * tile, tile)
+                res = jnp.dot(x[block], wup[:, pl.ds(start, tile)], preferred_element_type=jnp.float32)
+                res = res.astype(jnp.bfloat16)
+                for q in range(n_dp):
+                    up[part, q, s, from_z_at, :, j * tile : (j + 1) * tile] = res[
+                        q * cap : (q + 1) * cap
+                    ]
+
+    def up_to_core(s):
+        return [send(up.at[:, 1 - c + 2 * a, s], up_near.at[a, s], core) for a in range(2)]
+
+    def up_to_cross(s):
+        @pl.loop(0, n_z)
+        def _(m):
+            for a in range(2):
+                total = up[1 - h, c + 2 * a, s, m].astype(jnp.float32) + up_near[
+                    a, s, 1 - h, m
+                ].astype(jnp.float32)
+                up[1 - h, c + 2 * a, s, m] = total.astype(jnp.bfloat16)
+
+        return [send(up.at[1 - h, c + 2 * a, s], up_cross.at[a, s], cross) for a in range(2)]
+
+    step = 32
+
+    def pair_sum(first, end):
+        @pl.loop(first * (piece // step), end * (piece // step))
+        def _(i):
+            rows = pl.ds(pl.multiple_of(i * step, step), step)
+            total = g_own[0, rows].astype(jnp.float32) + g_near[0, rows].astype(jnp.float32)
+            g_own[0, rows] = total.astype(jnp.bfloat16)
+
+    def send_grad(k):
+        rows = pl.ds(k * piece, piece)
+        return send(g_own.at[0, rows], g_cross.at[rows], cross)
+
+    own_far, own_near, own_side = pass_on(t, (far, near, side))
+    loads[1].wait()
+    project(z, 1)
+    own_far.wait_recv()
+    far_near, far_side = pass_on(t4, (near, side))
+    project(z2, 1)
+    own_near.wait_recv()
+    (near_side,) = pass_on(t2, (side,))
+    project(z1, 1)
+    far_near.wait_recv()
+    (both_side,) = pass_on(flip(t2, 4), (side,))
+    project(z3, 1)
+
+    core_own = up_to_core(1)
+    loads[2].wait()
+    grad_core[0].wait_recv()
+    pair_sum(0, 1)
+    grad_cross = [send_grad(0)]
+    own_side.wait_recv()
+    project(z, 0)
+    for copy in core_own:
+        copy.wait_recv()
+    cross_own = up_to_cross(1)
+    for copy, at in ((far_side, z2), (near_side, z1), (both_side, z3)):
+        copy.wait_recv()
+        project(at, 0)
+    core_other = up_to_core(0)
+    wd_core = send(wdown_hbm, wd.at[c], core)
+    grad_core.append(send(grad_hbm.at[0, share_of(p1)], g_near.at[1], core))
+    for copy in core_other:
+        copy.wait_recv()
+    cross_other = up_to_cross(0)
+
+    pair_sum(1, CHUNKS)
+
+    loads[3].wait()
+    wd_core.wait_recv()
+    width = 256
+
+    def expert(s):
+        @pl.loop(0, n_z)
+        def _(m):
+            for a in range(2):
+                pre = (
+                    up[h, c + 2 * a, s, m].astype(jnp.float32)
+                    + up_near[a, s, h, m].astype(jnp.float32)
+                    + up_cross[a, s, m].astype(jnp.float32)
+                )
+                act = 0.5 * pre * (1.0 + lax.erf(pre * 0.7071067811865476))
+                hid[rows_of(2 * m + a), :] = act.astype(jnp.bfloat16)
+
+        @pl.loop(0, out.shape[4] // width)
+        def _(j):
+            cols = pl.ds(pl.multiple_of(j * width, width), width)
+            weight = wd[:, :, cols].reshape(2 * share, width)
+            res = jnp.dot(hid[...], weight, preferred_element_type=jnp.float32)
+            out[s, :, :, :, cols] = res.reshape(n_z, 2, cap, width).astype(jnp.bfloat16)
+
+    for copy in cross_own:
+        copy.wait_recv()
+    expert(1)
+    for copy in cross_other:
+        copy.wait_recv()
+    for k in range(1, CHUNKS):
+        grad_cross.append(send_grad(k))
+    expert(0)
+
+    y_copies = [
+        send(out.at[0, at], from_y.at[slot], side) for slot, at in enumerate((z3, z2, z1, z))
+    ]
+    loads[4].wait()
+    grad_core[1].wait_recv()
+
+    def finish_grad(k):
+        grad_cross[k].wait_recv()
+
+        @pl.loop(0, piece // step)
+        def _(i):
+            rows = pl.ds(pl.multiple_of(k * piece + i * step, step), step)
+            total = (
+                g_own[1, rows].astype(jnp.float32)
+                + g_near[1, rows].astype(jnp.float32)
+                + g_cross[rows].astype(jnp.float32)
+            )
+            gsum[rows, :] = total.astype(jnp.bfloat16)
+
+    def total_of(at, a, *others):
+        total = out[1, at, a].astype(jnp.float32)
+        for other in others:
+            total += other[a].astype(jnp.float32)
+        return total
+
+    def merge(at, *others):
+        for a in range(2):
+            out[1, at, a] = total_of(at, a, *others).astype(jnp.bfloat16)
+
+    y_copies[0].wait_recv()
+    merge(z3, from_y.at[0])
+    z_first = send(out.at[1, z3], from_z.at[0], near)
+    y_copies[1].wait_recv()
+    z_first.wait_recv()
+    merge(z2, from_y.at[1], from_z.at[0])
+    z_far = send(out.at[1, z2], from_far, far)
+    y_copies[2].wait_recv()
+    merge(z1, from_y.at[2])
+    z_second = send(out.at[1, z1], from_z.at[1], near)
+    for k in range(CHUNKS // 2):
+        finish_grad(k)
+    y_copies[3].wait_recv()
+    z_second.wait_recv()
+    z_far.wait_recv()
+    last = (from_y.at[3], from_z.at[1], from_far)
+    fin_out[...] = total_of(z, 1 - h, *last).astype(jnp.bfloat16)
+    fin = send(fin_out, fin_in, cross)
+    for k in range(CHUNKS // 2, CHUNKS):
+        finish_grad(k)
+    fin.wait_recv()
+    owned[...] = total_of(z, h, *last) + fin_in[...].astype(jnp.float32)
+
+    for copy in sent:
+        copy.wait_send()
+    assert used[0] == send_sem.shape[0]
+
+
+def layer(n_dp, n_tensor, pk, w_up, w_down, grad_parts):
+    cap, depth = pk.shape[1:]
+    hidden = w_up.shape[1]
+    share, model = w_down.shape
+    half = jnp.bfloat16
+    copies = 29 + CHUNKS
+    n_z = n_tensor // 2
+    scratch = [
+        pltpu.VMEM((n_tensor, n_dp * cap, depth), half),
+        pltpu.VMEM((depth, hidden), half),
+        pltpu.VMEM((2, n_dp, 2, n_z, cap, hidden // 2), half),
+        pltpu.VMEM((2, 2, 2, n_z, cap, hidden // 2), half),
+        pltpu.VMEM((2, 2, n_z, cap, hidden // 2), half),
+        pltpu.VMEM((2 * n_z * cap, hidden // 2), half),
+        pltpu.VMEM((2, share, model), half),
+        pltpu.VMEM((2, n_z, 2, cap, model), half),
+        pltpu.VMEM((n_z, 2, cap, model), half),
+        pltpu.VMEM((2, 2, cap, model), half),
+        pltpu.VMEM((2, cap, model), half),
+        pltpu.VMEM((cap, model), half),
+        pltpu.VMEM((cap, model), half),
+        pltpu.VMEM((2, share, model), half),
+        pltpu.VMEM((2, share, model), half),
+        pltpu.VMEM((share, model), half),
+        pltpu.SemaphoreType.DMA((copies,)),
+        pltpu.SemaphoreType.DMA((copies,)),
+        pltpu.SemaphoreType.DMA((5,)),
+    ]
+    flops = 2 * n_tensor * n_dp * cap * depth * hidden + 2 * n_tensor * cap * hidden * model
+    return pl.pallas_call(
+        functools.partial(layer_kernel, n_dp, n_tensor),
+        out_shape=(
+            jax.ShapeDtypeStruct((cap, model), jnp.float32),
+            jax.ShapeDtypeStruct((share, model), half),
+        ),
+        in_specs=[pl.BlockSpec(memory_space=pltpu.VMEM)] + [pl.BlockSpec(memory_space=pl.ANY)] * 3,
+        out_specs=(pl.BlockSpec(memory_space=pltpu.VMEM), pl.BlockSpec(memory_space=pltpu.VMEM)),
+        scratch_shapes=scratch,
+        cost_estimate=pl.CostEstimate(
+            flops=flops, bytes_accessed=40 * share * model, transcendentals=n_tensor * cap * hidden
+        ),
+        compiler_params=pltpu.CompilerParams(
+            collective_id=0, has_side_effects=True, vmem_limit_bytes=VMEM_BYTES
+        ),
+    )(pk, w_up, w_down, grad_parts)
+
+
+def local_kernel(n_dp, n_tensor, tokens, routes, router, w_up, w_down, grad_parts, master, moment_one, moment_two):
+    routed, gating = gating_of(tokens, routes, router)
+    slot_index = jnp.cumsum(routed.astype(jnp.int32)) - 1
+    slot_iota = jnp.arange(CAP, dtype=jnp.int32)
+    picks = ((slot_index[None, :] == slot_iota[:, None]) & routed[None, :]).astype(jnp.bfloat16)
+    picked_rows = jnp.dot(picks, tokens, preferred_element_type=jnp.float32).astype(jnp.bfloat16)
+    pk = picked_rows.reshape(CAP, n_dp, -1).transpose(1, 0, 2)
+    owned, grad_total = layer(n_dp, n_tensor, pk, w_up, w_down, grad_parts)
+    combined = jnp.take(owned, jnp.clip(slot_index, 0, CAP - 1), axis=0)
+    mixed = (combined * gating[:, None]).astype(jnp.bfloat16)
+    new_master, new_one, new_two = adam_step(
+        grad_total.astype(jnp.float32), master, moment_one, moment_two
+    )
     return (mixed, new_master, new_one, new_two)
 
 
@@ -76,8 +387,13 @@
         P(("tensor", "dp"), None),
         P(("tensor", "dp"), None),
     )
+    n_dp, n_tensor = mesh.shape["dp"], mesh.shape["tensor"]
+    if (n_dp, n_tensor) == (4, 8):
+        body = functools.partial(local_kernel, n_dp, n_tensor)
+    else:
+        body = local
     return jax.shard_map(
-        local,
+        body,
         mesh=mesh,
         in_specs=placed,
         out_specs=(

time: 448 us -> 180 us (0.40)
  waiting for transfers between devices: 387 us -> 0 us
  Pallas kernels: 0 us -> 157 us
  matrix products: 28 us -> 1.34 us
  between operations: 13.9 us -> 0.69 us
    all_gather x3 -> x0, waiting for transfers between devices: 220 us -> none  [the longest x1 83.7 us: local(): lax.all_gather(w_down, 'dp', axis=0, tiled=True)]
    reduce_scatter x2 -> x0, waiting for transfers between devices: 165 us -> none  [the longest x1 97.2 us: local(): lax.psum_scatter(local_grad, 'dp', scatter_dimension=0, tiled=True)]
    pallas_call x0 -> x1, Pallas kernels: none -> 157 us  [layer(): pl.pallas_call(functools.partial(layer_kernel, n_dp, n_tensor), out_shape...]
    dot_general x2 -> x1, matrix products: 27.7 us -> 0.24 us  [local_kernel(): jnp.dot(picks, tokens, preferred_element_type=jnp.float32)]
  transfers between devices with their start and end apart: 5 -> 0, of which waited for: 5 -> 0; matrix products, arithmetic and copies ran while one was open for 1% -> 0% of each run, Pallas kernels for 0% -> 0%
where the time goes in v1:
time: 180 us; the launch traced here: 179 us
  Pallas kernels  157 us (87%)
  other arithmetic  15.9 us (9%)
  local copies, waits for them, and re-layouts  4.55 us (3%)
    pallas_call x1, Pallas kernels, layer(): pl.pallas_call(functools.partial(layer_kernel, n_dp, n_tensor), out_shape...  157 us
    sub x1, other arithmetic, adam_step(): new_master = master - learn_rate * (update + decay_rate * master)  12.8 us

profile of v1, /device:TPU:0, one launch (start us, length us, event | category | flops | bytes accessed | tf_op | source)
XLA Modules:
  0.0 179.3 jit_solution(12537391822446285326)
XLA Ops:
  0.6 0.0 copy-start
  0.6 0.8 slice_compare_fusion
  1.4 0.4 copy-done
  1.8 1.1 fusion.11
  2.9 0.7 select_reduce_fusion.1
  3.6 0.1 copy.33
  3.8 0.1 copy.32
  3.9 0.1 copy.36
  4.0 0.1 copy.37
  4.1 0.1 select_reduce_fusion
  4.2 0.1 or_reduce_fusion
  4.4 0.2 reduce-window.4
  4.5 0.1 fusion.3
  4.7 0.2 convolution_convert_fusion
  4.9 0.7 copy.44
  5.7 156.8 %shard_map.120 = (f32[48,3072]{1,0:T(8,128)}, bf16[512,3072]{1,0:T(8,128)(2,1)}) custom-call(bf16[4,48,768]{2,1,0:T(8,128)(2,1)} %bitcast.11, bf16[768,2048]{1,0:T(8,128)(2,1)} %wup_hbm.1, bf16[512,3072]{1,0:T(8,128)(2,1)} %wdown_hbm.1, bf16[1,2048,3072]{2,1,0:T(8,128)(2,1)} %grad_hbm.1), custom_call_target="tpu_custom_call" | custom-call | flops 9663676416 | bytes 62914560 | tf_op jit(solution)/shard_map/pallas_call | solution.py:344
  162.5 2.9 %gather_fusion = f32[128,3072]{1,0:T(8,128)S(1)} fusion(f32[48,3072]{1,0:T(8,128)} %get-tuple-element.6, s32[1024]{0:T(1024)S(1)} %pad_clamp_fusion), kind=kCustom, calls=%fused_computation | custom fusion | bytes 3146240 | tf_op jit(solution)/shard_map/jit(_take)/gather | solution.py:370
  165.5 1.1 multiply_convert_fusion
  166.6 12.8 %multiply_subtract_fusion = (f32[512,3072]{1,0:T(8,128)}, bf16[512,3072]{1,0:T(8,128)(2,1)}, f32[512,3072]{1,0:T(8,128)}) fusion(f32[512,3072]{1,0:T(8,128)} %param.15, bf16[512,3072]{1,0:T(8,128)(2,1)} %get-tuple-element.7, bf16[512,3072]{1,0:T(8,128)(2,1)} %param.16, f32[512,3072]{1,0:T(8,128)} %param.17), kind=kLoop, calls=%fused_computation.6 | loop fusion | flops 29884416 | bytes 34603008 | tf_op jit(solution)/shard_map/sub | solution.py:40
  (3 shorter events, 0.0 us)
Async XLA Ops:
  0.6 1.2 copy-start

commit v2 on v1

--- a/solution.py
+++ b/solution.py
@@ -85,18 +85,16 @@
     p = lax.axis_index("dp")
     t = lax.axis_index("tensor")
     c, h = lax.rem(p, 2), lax.div(p, 2)
-    z, y = lax.div(t, 2), lax.rem(t, 2)
+    y, low, high = lax.rem(t, 2), lax.rem(lax.div(t, 2), 2), lax.div(t, 4)
+    other = 1 - high
     p1, p2 = flip(p, 1), flip(p, 2)
     p3 = flip(p1, 2)
     t1, t2, t4 = flip(t, 1), flip(t, 2), flip(t, 4)
-    z1, z2 = flip(z, 1), flip(z, 2)
-    z3 = flip(z1, 2)
     core, cross, diag = (p1, t), (p2, t), (p3, t)
     side, near, far = (p, t1), (p, t2), (p, t4)
     cap = pk.shape[1]
     share = wdown_hbm.shape[0]
     piece = share // CHUNKS
-    n_z = n_tensor // 2
     used = [0]
     sent = []
 
@@ -136,7 +134,15 @@
     ]
     for load in loads:
         load.start()
-    grad_core = [send(grad_hbm.at[0, share_of(p3)], g_near.at[0], core)]
+    wd_core = send(wdown_hbm, wd.at[c], core)
+    early = CHUNKS // 4
+
+    def grad_to_core(first, end):
+        start = pl.multiple_of(p3 * share + first * piece, 16)
+        rows = pl.ds(start, (end - first) * piece)
+        return send(grad_hbm.at[0, rows], g_near.at[0, pl.ds(first * piece, (end - first) * piece)], core)
+
+    grad_first = grad_to_core(0, early)
 
     for copy in tok:
         copy.wait_recv()
@@ -147,8 +153,8 @@
 
     tile = 512
 
-    def project(from_z_at, s):
-        block = 2 * from_z_at + (y if s == 1 else 1 - y)
+    def project(s, e):
+        block = 4 * e + 2 * (low if s in (0, 2) else 1 - low) + (y if s in (2, 3) else 1 - y)
 
         @pl.loop(0, 2)
         def _(part):
@@ -157,7 +163,7 @@
                 res = jnp.dot(x[block], wup[:, pl.ds(start, tile)], preferred_element_type=jnp.float32)
                 res = res.astype(jnp.bfloat16)
                 for q in range(n_dp):
-                    up[part, q, s, from_z_at, :, j * tile : (j + 1) * tile] = res[
+                    up[part, q, s, e, :, j * tile : (j + 1) * tile] = res[
                         q * cap : (q + 1) * cap
                     ]
 
@@ -165,7 +171,7 @@
         return [send(up.at[:, 1 - c + 2 * a, s], up_near.at[a, s], core) for a in range(2)]
 
     def up_to_cross(s):
-        @pl.loop(0, n_z)
+        @pl.loop(0, 2)
         def _(m):
             for a in range(2):
                 total = up[1 - h, c + 2 * a, s, m].astype(jnp.float32) + up_near[
@@ -190,45 +196,42 @@
 
     own_far, own_near, own_side = pass_on(t, (far, near, side))
     loads[1].wait()
-    project(z, 1)
+    project(2, high)
     own_far.wait_recv()
     far_near, far_side = pass_on(t4, (near, side))
-    project(z2, 1)
     own_near.wait_recv()
     (near_side,) = pass_on(t2, (side,))
-    project(z1, 1)
+    project(2, other)
     far_near.wait_recv()
     (both_side,) = pass_on(flip(t2, 4), (side,))
-    project(z3, 1)
-
-    core_own = up_to_core(1)
     loads[2].wait()
-    grad_core[0].wait_recv()
-    pair_sum(0, 1)
-    grad_cross = [send_grad(0)]
+    grad_first.wait_recv()
+    pair_sum(0, early)
+    grad_cross = [send_grad(k) for k in range(early)]
+
     own_side.wait_recv()
-    project(z, 0)
-    for copy in core_own:
-        copy.wait_recv()
-    cross_own = up_to_cross(1)
-    for copy, at in ((far_side, z2), (near_side, z1), (both_side, z3)):
-        copy.wait_recv()
-        project(at, 0)
-    core_other = up_to_core(0)
-    wd_core = send(wdown_hbm, wd.at[c], core)
-    grad_core.append(send(grad_hbm.at[0, share_of(p1)], g_near.at[1], core))
-    for copy in core_other:
-        copy.wait_recv()
-    cross_other = up_to_cross(0)
-
-    pair_sum(1, CHUNKS)
-
+    project(0, high)
+    far_side.wait_recv()
+    project(0, other)
+    core_0 = up_to_core(0)
+    core_2 = up_to_core(2)
+    project(3, high)
+    for copy in core_0:
+        copy.wait_recv()
+    cross_0 = up_to_cross(0)
+    project(3, other)
+    core_3 = up_to_core(3)
+    near_side.wait_recv()
+    project(1, high)
+    for copy in core_2:
+        copy.wait_recv()
+    cross_2 = up_to_cross(2)
     loads[3].wait()
     wd_core.wait_recv()
     width = 256
 
     def expert(s):
-        @pl.loop(0, n_z)
+        @pl.loop(0, 2)
         def _(m):
             for a in range(2):
                 pre = (
@@ -244,22 +247,43 @@
             cols = pl.ds(pl.multiple_of(j * width, width), width)
             weight = wd[:, :, cols].reshape(2 * share, width)
             res = jnp.dot(hid[...], weight, preferred_element_type=jnp.float32)
-            out[s, :, :, :, cols] = res.reshape(n_z, 2, cap, width).astype(jnp.bfloat16)
-
-    for copy in cross_own:
+            out[s, :, :, :, cols] = res.reshape(2, 2, cap, width).astype(jnp.bfloat16)
+
+    def send_out(s):
+        return [send(out.at[s, e], from_y.at[2 * s + k], side) for k, e in enumerate((other, high))]
+
+    for copy in cross_0:
+        copy.wait_recv()
+    expert(0)
+    y_copies = send_out(0)
+    both_side.wait_recv()
+    project(1, other)
+    core_1 = up_to_core(1)
+    grad_rest = grad_to_core(early, CHUNKS)
+    grad_last = send(grad_hbm.at[0, share_of(p1)], g_near.at[1], core)
+    for copy in core_1:
+        copy.wait_recv()
+    cross_1 = up_to_cross(1)
+    for copy in core_3:
+        copy.wait_recv()
+    cross_3 = up_to_cross(3)
+    for copy in cross_2:
+        copy.wait_recv()
+    expert(2)
+    for copy in cross_1:
         copy.wait_recv()
     expert(1)
-    for copy in cross_other:
-        copy.wait_recv()
-    for k in range(1, CHUNKS):
+
+    y_copies += send_out(1)
+    grad_rest.wait_recv()
+    for k in range(early, CHUNKS):
+        pair_sum(k, k + 1)
         grad_cross.append(send_grad(k))
-    expert(0)
-
-    y_copies = [
-        send(out.at[0, at], from_y.at[slot], side) for slot, at in enumerate((z3, z2, z1, z))
-    ]
+    for copy in cross_3:
+        copy.wait_recv()
+    expert(3)
     loads[4].wait()
-    grad_core[1].wait_recv()
+    grad_last.wait_recv()
 
     def finish_grad(k):
         grad_cross[k].wait_recv()
@@ -274,38 +298,40 @@
             )
             gsum[rows, :] = total.astype(jnp.bfloat16)
 
-    def total_of(at, a, *others):
-        total = out[1, at, a].astype(jnp.float32)
-        for other in others:
-            total += other[a].astype(jnp.float32)
+    def total_of(s, e, a, *others):
+        total = out[s, e, a].astype(jnp.float32)
+        for more in others:
+            total += more[a].astype(jnp.float32)
         return total
 
-    def merge(at, *others):
+    def merge(s, e, *others):
         for a in range(2):
-            out[1, at, a] = total_of(at, a, *others).astype(jnp.bfloat16)
-
-    y_copies[0].wait_recv()
-    merge(z3, from_y.at[0])
-    z_first = send(out.at[1, z3], from_z.at[0], near)
-    y_copies[1].wait_recv()
-    z_first.wait_recv()
-    merge(z2, from_y.at[1], from_z.at[0])
-    z_far = send(out.at[1, z2], from_far, far)
+            out[s, e, a] = total_of(s, e, a, *others).astype(jnp.bfloat16)
+
     y_copies[2].wait_recv()
-    merge(z1, from_y.at[2])
-    z_second = send(out.at[1, z1], from_z.at[1], near)
-    for k in range(CHUNKS // 2):
+    merge(3, other, from_y.at[2])
+    z_first = send(out.at[3, other], from_z.at[0], near)
+    for k in range(early):
         finish_grad(k)
     y_copies[3].wait_recv()
+    merge(3, high, from_y.at[3])
+    z_second = send(out.at[3, high], from_z.at[1], near)
+    y_copies[0].wait_recv()
+    z_first.wait_recv()
+    merge(2, other, from_y.at[0], from_z.at[0])
+    z_far = send(out.at[2, other], from_far, far)
+    for k in range(early, CHUNKS // 2):
+        finish_grad(k)
+    y_copies[1].wait_recv()
     z_second.wait_recv()
     z_far.wait_recv()
-    last = (from_y.at[3], from_z.at[1], from_far)
-    fin_out[...] = total_of(z, 1 - h, *last).astype(jnp.bfloat16)
+    last = (from_y.at[1], from_z.at[1], from_far)
+    fin_out[...] = total_of(2, high, 1 - h, *last).astype(jnp.bfloat16)
     fin = send(fin_out, fin_in, cross)
     for k in range(CHUNKS // 2, CHUNKS):
         finish_grad(k)
     fin.wait_recv()
-    owned[...] = total_of(z, h, *last) + fin_in[...].astype(jnp.float32)
+    owned[...] = total_of(2, high, h, *last) + fin_in[...].astype(jnp.float32)
 
     for copy in sent:
         copy.wait_send()
@@ -317,18 +343,18 @@
     hidden = w_up.shape[1]
     share, model = w_down.shape
     half = jnp.bfloat16
-    copies = 29 + CHUNKS
-    n_z = n_tensor // 2
+    copies = 38 + CHUNKS
+    wide = (2, cap, hidden // 2)
     scratch = [
         pltpu.VMEM((n_tensor, n_dp * cap, depth), half),
         pltpu.VMEM((depth, hidden), half),
-        pltpu.VMEM((2, n_dp, 2, n_z, cap, hidden // 2), half),
-        pltpu.VMEM((2, 2, 2, n_z, cap, hidden // 2), half),
-        pltpu.VMEM((2, 2, n_z, cap, hidden // 2), half),
-        pltpu.VMEM((2 * n_z * cap, hidden // 2), half),
+        pltpu.VMEM((2, n_dp, 4) + wide, half),
+        pltpu.VMEM((2, 4, 2) + wide, half),
+        pltpu.VMEM((2, 4) + wide, half),
+        pltpu.VMEM((4 * cap, hidden // 2), half),
         pltpu.VMEM((2, share, model), half),
-        pltpu.VMEM((2, n_z, 2, cap, model), half),
-        pltpu.VMEM((n_z, 2, cap, model), half),
+        pltpu.VMEM((4, 2, 2, cap, model), half),
+        pltpu.VMEM((4, 2, cap, model), half),
         pltpu.VMEM((2, 2, cap, model), half),
         pltpu.VMEM((2, cap, model), half),
         pltpu.VMEM((cap, model), half),

time: 180 us -> 174 us (0.967)
  Pallas kernels: 157 us -> 151 us
    pallas_call x1, Pallas kernels: 157 us -> 151 us  [layer(): pl.pallas_call(functools.partial(layer_kernel, n_dp, n_tensor), out_shape...]
where the time goes in v2:
time: 174 us; the launch traced here: 173 us
  Pallas kernels  151 us (87%)
  other arithmetic  15.9 us (9%)
  local copies, waits for them, and re-layouts  4.55 us (3%)
    pallas_call x1, Pallas kernels, layer(): pl.pallas_call(functools.partial(layer_kernel, n_dp, n_tensor), out_shape...  151 us
    sub x1, other arithmetic, adam_step(): new_master = master - learn_rate * (update + decay_rate * master)  12.8 us

profile of v2, /device:TPU:0, one launch (start us, length us, event | category | flops | bytes accessed | tf_op | source)
XLA Modules:
  0.0 173.2 jit_solution(4519493664380134573)
XLA Ops:
  0.6 0.0 copy-start
  0.6 0.8 slice_compare_fusion
  1.4 0.4 copy-done
  1.8 1.1 fusion.11
  2.9 0.7 select_reduce_fusion.1
  3.6 0.1 copy.33
  3.8 0.1 copy.32
  3.9 0.1 copy.36
  4.0 0.1 copy.37
  4.1 0.1 select_reduce_fusion
  4.2 0.1 or_reduce_fusion
  4.4 0.2 reduce-window.4
  4.5 0.1 fusion.3
  4.7 0.2 convolution_convert_fusion
  4.9 0.7 copy.44
  5.7 150.7 %shard_map.120 = (f32[48,3072]{1,0:T(8,128)}, bf16[512,3072]{1,0:T(8,128)(2,1)}) custom-call(bf16[4,48,768]{2,1,0:T(8,128)(2,1)} %bitcast.11, bf16[768,2048]{1,0:T(8,128)(2,1)} %wup_hbm.1, bf16[512,3072]{1,0:T(8,128)(2,1)} %wdown_hbm.1, bf16[1,2048,3072]{2,1,0:T(8,128)(2,1)} %grad_hbm.1), custom_call_target="tpu_custom_call" | custom-call | flops 9663676416 | bytes 62914560 | tf_op jit(solution)/shard_map/pallas_call | solution.py:370
  156.4 2.9 %gather_fusion = f32[128,3072]{1,0:T(8,128)S(1)} fusion(f32[48,3072]{1,0:T(8,128)} %get-tuple-element.6, s32[1024]{0:T(1024)S(1)} %pad_clamp_fusion), kind=kCustom, calls=%fused_computation | custom fusion | bytes 3146240 | tf_op jit(solution)/shard_map/jit(_take)/gather | solution.py:396
  159.4 1.1 multiply_convert_fusion
  160.5 12.8 %multiply_subtract_fusion = (f32[512,3072]{1,0:T(8,128)}, bf16[512,3072]{1,0:T(8,128)(2,1)}, f32[512,3072]{1,0:T(8,128)}) fusion(f32[512,3072]{1,0:T(8,128)} %param.15, bf16[512,3072]{1,0:T(8,128)(2,1)} %get-tuple-element.7, bf16[512,3072]{1,0:T(8,128)(2,1)} %param.16, f32[512,3072]{1,0:T(8,128)} %param.17), kind=kLoop, calls=%fused_computation.6 | loop fusion | flops 29884416 | bytes 34603008 | tf_op jit(solution)/shard_map/sub | solution.py:40
  (3 shorter events, 0.0 us)
Async XLA Ops:
  0.6 1.2 copy-start

commit v3 on v2

--- a/solution.py
+++ b/solution.py
@@ -221,6 +221,8 @@
     cross_0 = up_to_cross(0)
     project(3, other)
     core_3 = up_to_core(3)
+    grad_rest = grad_to_core(early, CHUNKS)
+    grad_last = send(grad_hbm.at[0, share_of(p1)], g_near.at[1], core)
     near_side.wait_recv()
     project(1, high)
     for copy in core_2:
@@ -250,7 +252,11 @@
             out[s, :, :, :, cols] = res.reshape(2, 2, cap, width).astype(jnp.bfloat16)
 
     def send_out(s):
-        return [send(out.at[s, e], from_y.at[2 * s + k], side) for k, e in enumerate((other, high))]
+        return [
+            send(out.at[s, e, a], from_y.at[2 * s + k, a], side)
+            for k, e in enumerate((other, high))
+            for a in (1 - h, h)
+        ]
 
     for copy in cross_0:
         copy.wait_recv()
@@ -259,8 +265,6 @@
     both_side.wait_recv()
     project(1, other)
     core_1 = up_to_core(1)
-    grad_rest = grad_to_core(early, CHUNKS)
-    grad_last = send(grad_hbm.at[0, share_of(p1)], g_near.at[1], core)
     for copy in core_1:
         copy.wait_recv()
     cross_1 = up_to_cross(1)
@@ -270,13 +274,16 @@
     for copy in cross_2:
         copy.wait_recv()
     expert(2)
+    grad_rest.wait_recv()
+    pair_sum(early, 2 * early)
     for copy in cross_1:
         copy.wait_recv()
+    for k in range(early, 2 * early):
+        grad_cross.append(send_grad(k))
     expert(1)
 
     y_copies += send_out(1)
-    grad_rest.wait_recv()
-    for k in range(early, CHUNKS):
+    for k in range(2 * early, CHUNKS):
         pair_sum(k, k + 1)
         grad_cross.append(send_grad(k))
     for copy in cross_3:
@@ -304,34 +311,47 @@
             total += more[a].astype(jnp.float32)
         return total
 
-    def merge(s, e, *others):
-        for a in range(2):
-            out[s, e, a] = total_of(s, e, a, *others).astype(jnp.bfloat16)
-
+    def merge(s, e, a, *others):
+        out[s, e, a] = total_of(s, e, a, *others).astype(jnp.bfloat16)
+
+    def to_near(slot, e, a):
+        merge(3, e, a, from_y.at[2 + slot])
+        return send(out.at[3, e, a], from_z.at[slot, a], near)
+
+    def to_far(a):
+        merge(2, other, a, from_y.at[0], from_z.at[0])
+        return send(out.at[2, other, a], from_far.at[a], far)
+
+    first, second = 1 - h, h
+    y_copies[4].wait_recv()
+    z_first = [to_near(0, other, first)]
+    y_copies[5].wait_recv()
+    z_first.append(to_near(0, other, second))
+    y_copies[0].wait_recv()
+    y_copies[1].wait_recv()
+    z_first[0].wait_recv()
+    z_far = [to_far(first)]
+    y_copies[6].wait_recv()
+    z_second = [to_near(1, high, first)]
+    z_first[1].wait_recv()
+    z_far.append(to_far(second))
+    y_copies[7].wait_recv()
+    z_second.append(to_near(1, high, second))
+    for k in range(2 * early):
+        finish_grad(k)
     y_copies[2].wait_recv()
-    merge(3, other, from_y.at[2])
-    z_first = send(out.at[3, other], from_z.at[0], near)
-    for k in range(early):
+    y_copies[3].wait_recv()
+    last = (from_y.at[1], from_z.at[1], from_far)
+    z_second[0].wait_recv()
+    z_far[0].wait_recv()
+    fin_out[...] = total_of(2, high, first, *last).astype(jnp.bfloat16)
+    fin = send(fin_out, fin_in, cross)
+    for k in range(2 * early, CHUNKS):
         finish_grad(k)
-    y_copies[3].wait_recv()
-    merge(3, high, from_y.at[3])
-    z_second = send(out.at[3, high], from_z.at[1], near)
-    y_copies[0].wait_recv()
-    z_first.wait_recv()
-    merge(2, other, from_y.at[0], from_z.at[0])
-    z_far = send(out.at[2, other], from_far, far)
-    for k in range(early, CHUNKS // 2):
-        finish_grad(k)
-    y_copies[1].wait_recv()
-    z_second.wait_recv()
-    z_far.wait_recv()
-    last = (from_y.at[1], from_z.at[1], from_far)
-    fin_out[...] = total_of(2, high, 1 - h, *last).astype(jnp.bfloat16)
-    fin = send(fin_out, fin_in, cross)
-    for k in range(CHUNKS // 2, CHUNKS):
-        finish_grad(k)
+    z_second[1].wait_recv()
+    z_far[1].wait_recv()
     fin.wait_recv()
-    owned[...] = total_of(2, high, h, *last) + fin_in[...].astype(jnp.float32)
+    owned[...] = total_of(2, high, second, *last) + fin_in[...].astype(jnp.float32)
 
     for copy in sent:
         copy.wait_send()
@@ -343,7 +363,7 @@
     hidden = w_up.shape[1]
     share, model = w_down.shape
     half = jnp.bfloat16
-    copies = 38 + CHUNKS
+    copies = 45 + CHUNKS
     wide = (2, cap, hidden // 2)
     scratch = [
         pltpu.VMEM((n_tensor, n_dp * cap, depth), half),
@@ -393,7 +413,9 @@
     picked_rows = jnp.dot(picks, tokens, preferred_element_type=jnp.float32).astype(jnp.bfloat16)
     pk = picked_rows.reshape(CAP, n_dp, -1).transpose(1, 0, 2)
     owned, grad_total = layer(n_dp, n_tensor, pk, w_up, w_down, grad_parts)
-    combined = jnp.take(owned, jnp.clip(slot_index, 0, CAP - 1), axis=0)
+    combined = lax.dot_general(
+        picks.astype(jnp.float32), owned, (((0,), (0,)), ((), ())), precision=lax.Precision.HIGHEST
+    )
     mixed = (combined * gating[:, None]).astype(jnp.bfloat16)
     new_master, new_one, new_two = adam_step(
         grad_total.astype(jnp.float32), master, moment_one, moment_two

time: 174 us -> 165 us (0.948)
  Pallas kernels: 151 us -> 144 us
  matrix products: 1.34 us -> 4.14 us
  local copies, waits for them, and re-layouts: 4.55 us -> 1.98 us
  other arithmetic: 15.9 us -> 13.6 us
    pallas_call x1, Pallas kernels: 151 us -> 144 us  [layer(): pl.pallas_call(functools.partial(layer_kernel, n_dp, n_tensor), out_shape...]
    gather x1 -> x0, local copies, waits for them, and re-layouts: 2.92 us -> none  [local_kernel(): combined = jnp.take(owned, jnp.clip(slot_index, 0, CAP - 1), axis=0)]
    dot_general x0 -> x1, matrix products: none -> 2.79 us  [local_kernel(): lax.dot_general(picks.astype(jnp.float32), owned, (((0,), (0,)), ((), ())...]
where the time goes in v3:
time: 165 us
  Pallas kernels  144 us (87%)
  other arithmetic  13.6 us (8%)
  matrix products  4.14 us (3%)
  local copies, waits for them, and re-layouts  1.98 us (1%)
    pallas_call x1, Pallas kernels, layer(): pl.pallas_call(functools.partial(layer_kernel, n_dp, n_tensor), out_shape...  144 us
    sub x1, other arithmetic, adam_step(): new_master = master - learn_rate * (update + decay_rate * master)  11.8 us

profile of v3, /device:TPU:0, one launch (start us, length us, event | category | flops | bytes accessed | tf_op | source)
XLA Modules:
  0.0 164.7 jit_solution(5410636734036845872)
XLA Ops:
  0.6 0.0 copy-start
  0.6 1.1 copy-done
  1.8 1.1 fusion.14
  2.9 0.7 select_reduce_fusion
  3.6 0.8 fusion.11
  4.4 0.1 copy.20
  4.5 0.2 reduce-window.8
  4.6 0.1 add_reduce_fusion
  4.8 0.3 convolution_convert_fusion
  5.0 0.7 copy.24
  5.8 0.0 copy-start.1
  5.8 144.3 %shard_map.120 = (f32[48,3072]{1,0:T(8,128)}, bf16[512,3072]{1,0:T(8,128)(2,1)}) custom-call(bf16[4,48,768]{2,1,0:T(8,128)(2,1)} %bitcast.15, bf16[768,2048]{1,0:T(8,128)(2,1)} %wup_hbm.1, bf16[512,3072]{1,0:T(8,128)(2,1)} %wdown_hbm.1, bf16[1,2048,3072]{2,1,0:T(8,128)(2,1)} %grad_hbm.1), custom_call_target="tpu_custom_call" | custom-call | flops 9663676416 | bytes 62914560 | tf_op jit(solution)/shard_map/pallas_call | solution.py:390
  150.1 2.8 %fusion.3 = bf16[128,3072]{1,0:T(8,128)(2,1)} fusion(f32[48,3072]{1,0:T(8,128)} %get-tuple-element.6, f32[128]{0:T(128)S(1)} %get-tuple-element.11, s32[128]{0:T(128)S(1)} %add_reduce_fusion, pred[128]{0:T(512)(128)(4,1)S(1)} %bitcast.17), kind=kOutput, calls=%fused_computation.7 | convolution fusion | flops 227291136 | bytes 1377408 | tf_op jit(solution)/shard_map/dot_general | solution.py:416
  152.8 0.0 copy-done.1
  152.8 11.8 %multiply_subtract_fusion = (f32[512,3072]{1,0:T(8,128)}, bf16[512,3072]{1,0:T(8,128)(2,1)}, f32[512,3072]{1,0:T(8,128)}) fusion(f32[512,3072]{1,0:T(8,128)} %param.15, bf16[512,3072]{1,0:T(8,128)(2,1)} %get-tuple-element.7, bf16[512,3072]{1,0:T(8,128)(2,1)S(1)} %copy-done.1, f32[512,3072]{1,0:T(8,128)} %param.17), kind=kLoop, calls=%fused_computation.5 | loop fusion | flops 29884416 | bytes 34603008 | tf_op jit(solution)/shard_map/sub | solution.py:40
  (1 shorter events, 0.0 us)
Async XLA Ops:
  0.6 1.1 copy-start
  5.8 147.1 %copy-start.1 = (bf16[512,3072]{1,0:T(8,128)(2,1)S(1)}, bf16[512,3072]{1,0:T(8,128)(2,1)}, u32[]{:S(2)}) copy-start(bf16[512,3072]{1,0:T(8,128)(2,1)} %param.16) | copy-start | bytes 9437188
